TPU v7x, 32 devices: a whole 2x2x4 slice. The times are simulated.
32 devices in a mesh: lag: 4 (over x, core), row: 8 (over z, y).
Axes of the slice: x: 2, y: 2, z: 4, core: 2. Of those that a mesh axis runs over, the one named last changes fastest.
Arguments:
- currents: bfloat16 [512, 4096], P('lag', 'row'), may hold values from -6 to 6
- panels: bfloat16 [4, 4096, 4096], P('lag', 'row'), may hold values from -0.09375 to 0.09375
- excitation: float32 [512, 4096], P('lag', 'row'), may hold values from -6 to 6
Outputs:
- residual: float32 [512, 4096], P('lag', 'row')
All inputs are finite; a program needn't handle non-finite values.
Results may differ from a plain program's by a relative error of at most 0.0003.
Values may be sent and summed in bfloat16 or wider, within the bound.
A program may use at most 64 MiB of HBM per device.

v0:
```python
import functools

import jax
import jax.numpy as jnp
from jax import lax
from jax.experimental import pallas as pl
from jax.experimental.pallas import tpu as pltpu
from jax.sharding import PartitionSpec as P

MESH = pl.DeviceIdType.MESH
PAD = 16
PIECES = 2


def kernel(planes, cur_ref, pan_ref, exc_ref, out_ref, buf, pan, exc, acc, give, got, over, landed,
           send_sem, own_sem, sib_sem, half_sem, load_sem, give_sem, over_sem):
    lag, row = lax.axis_index("lag"), lax.axis_index("row")
    x, c = lag // 2, lag % 2
    z, y = row // 2, row % 2
    nx, ny = 1 - x, 1 - y
    steps, width = cur_ref.shape
    rows = 2 * planes
    half = steps // 2
    to_x, to_y = (2 * nx + c, row), (lag, 2 * z + ny)
    to_s = (2 * x + 1 - c, row)
    to_up, to_down = (lag, row + 2), (lag, row - 2)
    has_up, has_down = z + 1 < planes, z >= 1

    barrier = pltpu.get_barrier_semaphore()

    def greet(device):
        pl.semaphore_signal(barrier, inc=1, device_id=device, device_id_type=MESH)

    greet(to_s)
    greet(to_x)
    greet(to_y)
    pl.when(has_up)(lambda: greet(to_up))
    pl.when(has_down)(lambda: greet(to_down))

    loads = [pltpu.make_async_copy(cur_ref, buf.at[row, lag], load_sem.at[0]),
             pltpu.make_async_copy(exc_ref, exc, load_sem.at[1])]
    for r in range(rows):
        loads.append(pltpu.make_async_copy(
            pan_ref.at[0, :, pl.ds(r * width, width)], pan.at[r], load_sem.at[2 + r]))
    for load in loads:
        load.start()

    pl.semaphore_wait(barrier, 3 + has_up.astype(jnp.int32) + has_down.astype(jnp.int32))

    sent = []

    def send(src, dst, sem, device, guards=()):
        slot = len(sent)

        def make():
            return pltpu.make_async_remote_copy(
                src_ref=src(), dst_ref=dst(), send_sem=send_sem.at[slot], recv_sem=sem(),
                device_id=device, device_id_type=MESH)

        sent.append((guards, make))
        make().start()

    def place(bx, by, bz):
        return lambda: buf.at[2 * bz + by, 2 * bx + c]

    def mark(sems, bx, by, bz):
        return lambda: sems.at[(2 * bz + by) * 2 + bx]

    def arrive(dst, sem):
        pltpu.make_async_remote_copy(
            src_ref=dst, dst_ref=dst, send_sem=send_sem.at[0], recv_sem=sem,
            device_id=to_s, device_id_type=MESH).wait_recv()

    def forward(bx, by, bz, device, guards=(), src=None):
        send(src or place(bx, by, bz), place(bx, by, bz), mark(own_sem, bx, by, bz), device, guards)

    def share(bx, by, bz, guards=(), src=None):
        send(src or place(bx, by, bz), place(bx, by, bz), mark(sib_sem, bx, by, bz), to_s, guards)

    def take(bx, by, bz):
        arrive(place(bx, by, bz)(), mark(own_sem, bx, by, bz)())

    def part(bx, by, bz, h):
        return lambda: buf.at[2 * bz + by, 2 * bx + c, pl.ds(h * half, half)]

    def when(guard, body):
        pl.when(guard)(body)

    mine = lambda: cur_ref
    forward(x, y, z, to_x, src=mine)
    forward(x, y, z, to_y, src=mine)
    when(has_up, lambda: forward(x, y, z, to_up, (has_up,), mine))
    when(has_down, lambda: forward(x, y, z, to_down, (has_down,), mine))
    share(x, y, z, src=mine)

    acc[...] = jnp.zeros_like(acc)

    def go_on(bx, by, bz, up, guard):
        g, device = (has_up, to_up) if up else (has_down, to_down)
        when(g, lambda: forward(bx, by, bz, device, (guard, g)))

    def column(up, d):
        bz = z - d if up else z + d
        guard = bz >= 0 if up else bz < planes

        def body():
            take(x, y, bz)
            if d < planes - 1:
                go_on(x, y, bz, up, guard)
            forward(x, y, bz, to_x, (guard,))
            forward(x, y, bz, to_y, (guard,))
            share(x, y, bz, (guard,))

        when(guard, body)

    last = planes - 1 if planes >= 3 else planes

    def diagonal(up, d):
        bz = z - d if up else z + d
        guard = bz >= 0 if up else bz < planes

        def body():
            if d < last:
                take(nx, ny, bz)
                if d + 1 < last:
                    go_on(nx, ny, bz, up, guard)
            else:
                for h in (0, 1):
                    arrive(part(nx, ny, bz, h)(), half_sem.at[2 + h])
            share(nx, ny, bz, (guard,))

        when(guard, body)

    def sides(up, d):
        bz = z - d if up else z + d
        guard = bz >= 0 if up else bz < planes

        def body():
            take(nx, y, bz)
            if d == last:
                send(part(nx, y, bz, 0), part(nx, y, bz, 0), lambda: half_sem.at[2], to_y, (guard,))
            share(nx, y, bz, (guard,))
            take(x, ny, bz)
            if d == last:
                send(part(x, ny, bz, 1), part(x, ny, bz, 1), lambda: half_sem.at[3], to_x, (guard,))
            share(x, ny, bz, (guard,))

        when(guard, body)

    def multiply(by, bz):
        for bx in (0, 1):
            arrive(buf.at[2 * bz + by, 2 * bx + 1 - c], mark(sib_sem, bx, by, bz)())
        r = 2 * bz + by
        lhs = buf[r].reshape(-1, width)
        acc[pl.ds(PAD, lhs.shape[0]), :] += lax.dot_general(
            lhs, pan[r], (((1,), (1,)), ((), ())), preferred_element_type=jnp.float32)

    def multiply_plane(up, d):
        bz = z - d if up else z + d
        guard = bz >= 0 if up else bz < planes

        def body():
            @pl.loop(0, 2)
            def _(by):
                multiply(by, bz)

        when(guard, body)

    take(nx, y, z)
    send(part(nx, y, z, 0), part(nx, y, z, 0), lambda: half_sem.at[0], to_y)
    share(nx, y, z)
    take(x, ny, z)
    send(part(x, ny, z, 1), part(x, ny, z, 1), lambda: half_sem.at[1], to_x)
    share(x, ny, z)
    if planes > 1:
        column(True, 1)
        column(False, 1)
    for h in (0, 1):
        arrive(part(nx, ny, z, h)(), half_sem.at[h])
    when(has_up, lambda: forward(nx, ny, z, to_up, (has_up,)))
    when(has_down, lambda: forward(nx, ny, z, to_down, (has_down,)))
    share(nx, ny, z)
    def both(step, d):
        if 1 <= d < planes:
            step(True, d)
            step(False, d)

    both(column, 2)
    if last > 1:
        both(diagonal, 1)
    for load in loads:
        load.wait()

    @pl.loop(0, 2)
    def _(by):
        multiply(by, z)

    both(column, 3)
    if last > 2:
        both(diagonal, 2)
    both(sides, 1)
    if last > 1:
        both(multiply_plane, 1)
    for d in range(2, planes):
        if d + 2 < planes:
            both(column, d + 2)
        if d + 1 < last:
            both(diagonal, d + 1)
        both(sides, d)
        if d == last:
            if d > 2:
                both(multiply_plane, d - 1)
            both(diagonal, d)
            both(multiply_plane, d)
        elif d + 1 < last:
            both(multiply_plane, d)
    piece = steps // PIECES

    def shifted(bx, core, p):
        first = pl.multiple_of(PAD - 8 + (2 * bx + core) * steps + p * piece, 8)
        window = acc[pl.ds(first, piece + 8), :]
        return pltpu.roll(window, piece + lag, 0)[:piece]

    order = [(0, p) for p in range(PIECES)] + [(1, p) for p in range(PIECES)]
    for j, p in order:
        give[j, p] = shifted(nx if j == 0 else x, 1 - c, p)
        send(lambda j=j, p=p: give.at[j, p], lambda j=j, p=p: got.at[j, p],
             lambda j=j, p=p: give_sem.at[j * PIECES + p], to_s)
    for p in range(PIECES):
        arrive(got.at[0, p], give_sem.at[p])
        over[p] = shifted(nx, c, p) + got[0, p]
        send(lambda p=p: over.at[p], lambda p=p: landed.at[p], lambda p=p: over_sem.at[p], to_x)
    for p in range(PIECES):
        arrive(got.at[1, p], give_sem.at[PIECES + p])
        at = pl.ds(p * piece, piece)
        exc[at, :] = exc[at, :] - (shifted(x, c, p) + got[1, p])
    for p in range(PIECES):
        arrive(landed.at[p], over_sem.at[p])
        at = pl.ds(p * piece, piece)
        out_ref[at, :] = exc[at, :] - landed[p]

    for guards, make in sent:
        if guards:
            g = functools.reduce(jnp.logical_and, guards)
            pl.when(g)(lambda make=make: make().wait_send())
        else:
            make().wait_send()


def fused(currents, panels, excitation):
    steps, width = currents.shape
    count = panels.shape[1]
    lags, rows = lax.axis_size("lag"), lax.axis_size("row")
    planes = rows // 2
    hbm_spec = pl.BlockSpec(memory_space=pltpu.HBM)
    dma = pltpu.SemaphoreType.DMA
    piece = steps // PIECES
    return pl.pallas_call(
        functools.partial(kernel, planes),
        out_shape=jax.ShapeDtypeStruct(excitation.shape, jnp.float32),
        in_specs=[hbm_spec] * 3,
        out_specs=pl.BlockSpec(memory_space=pltpu.VMEM),
        scratch_shapes=[
            pltpu.VMEM((rows, lags, steps, width), jnp.bfloat16),
            pltpu.VMEM((rows, count, width), jnp.bfloat16),
            pltpu.VMEM((steps, count), jnp.float32),
            pltpu.VMEM((PAD + lags * steps, count), jnp.float32),
            pltpu.VMEM((2, PIECES, piece, count), jnp.float32),
            pltpu.VMEM((2, PIECES, piece, count), jnp.float32),
            pltpu.VMEM((PIECES, piece, count), jnp.float32),
            pltpu.VMEM((PIECES, piece, count), jnp.float32),
            dma((24 + 20 * planes + 3 * PIECES,)),
            dma((2 * rows,)),
            dma((2 * rows,)),
            dma((4,)),
            dma((2 + rows,)),
            dma((2 * PIECES,)),
            dma((PIECES,)),
        ],
        compiler_params=pltpu.CompilerParams(
            collective_id=0, has_side_effects=True, vmem_limit_bytes=64 * 2**20),
        cost_estimate=pl.CostEstimate(
            flops=2 * lags * steps * width * rows * count,
            bytes_accessed=panels.size * 2, transcendentals=0),
    )(currents, panels, excitation)


def plain(currents, panels, excitation):
    gathered = lax.all_gather(currents, "row", axis=1, tiled=True)
    block_len = currents.shape[0]
    lag_total = lax.axis_size("lag")
    lag_index = lax.axis_index("lag")
    all_times = block_len * lag_total
    running = jnp.zeros((all_times + lag_total, panels.shape[1]), jnp.float32)
    product = lax.dot_general(
        lax.all_gather(gathered, "lag", axis=0, tiled=True),
        panels[0],
        (((1,), (1,)), ((), ())),
        preferred_element_type=jnp.float32,
    )
    running = lax.dynamic_update_slice_in_dim(running, product, lag_index, 0)
    field = lax.psum_scatter(running[:all_times], "lag", scatter_dimension=0, tiled=True)
    return excitation - field


def solution(mesh):
    paired = mesh.shape["lag"] == 4 and mesh.shape["row"] % 2 == 0
    return jax.shard_map(
        fused if paired else plain,
        mesh=mesh,
        in_specs=(P("lag", "row"), P("lag", "row", None), P("lag", "row")),
        out_specs=P("lag", "row"),
        check_vma=False,
    )
```

profile of v0, /device:TPU:0, one launch (start us, length us, event | category | flops | bytes accessed | tf_op | source)
XLA Modules:
  0.0 42.0 jit_solution(3282569305063406464)
XLA Ops:
  0.0 40.3 %shard_map.37 = f32[128,512]{1,0:T(8,128)} custom-call(bf16[128,512]{1,0:T(8,128)(2,1)} %cur_ref.1, bf16[1,512,4096]{2,1,0:T(8,128)(2,1)} %pan_ref.1, f32[128,512]{1,0:T(8,128)} %exc_ref.1), custom_call_target="tpu_custom_call" | custom-call | flops 2147483648 | bytes 4194304 | tf_op jit(solution)/shard_map/pallas_call | solution.py:258
  40.3 1.7 %copy.5 = f32[128,512]{1,0:T(8,128)} copy(f32[128,512]{1,0:T(8,128)} %shard_map.37) | data formatting | bytes 524288
where the time goes:
time: 42.2 us; the launch traced here: 42 us
  Pallas kernels  40.3 us (95%)
  local copies, waits for them, and re-layouts  1.67 us (4%)
    pallas_call x1, Pallas kernels, fused(): pl.pallas_call(functools.partial(kernel, planes), out_shape=jax.ShapeDtyp...  40.3 us
    unnamed x1, local copies, waits for them, and re-layouts  1.67 us

commit v1 on v0

--- a/solution.py
+++ b/solution.py
@@ -9,11 +9,12 @@
 
 MESH = pl.DeviceIdType.MESH
 PAD = 16
-PIECES = 2
+PIECES = 4
+HALVES = (0, 1)
 
 
 def kernel(planes, cur_ref, pan_ref, exc_ref, out_ref, buf, pan, exc, acc, give, got, over, landed,
-           send_sem, own_sem, sib_sem, half_sem, load_sem, give_sem, over_sem):
+           send_sem, own_sem, sib_sem, load_sem, give_sem, over_sem):
     lag, row = lax.axis_index("lag"), lax.axis_index("row")
     x, c = lag // 2, lag % 2
     z, y = row // 2, row % 2
@@ -63,101 +64,106 @@
     def place(bx, by, bz):
         return lambda: buf.at[2 * bz + by, 2 * bx + c]
 
-    def mark(sems, bx, by, bz):
-        return lambda: sems.at[(2 * bz + by) * 2 + bx]
+    def part(bx, by, bz, h):
+        return lambda: buf.at[2 * bz + by, 2 * bx + c, pl.ds(h * half, half)]
+
+    def part_mark(bx, by, bz, h):
+        return lambda: own_sem.at[((2 * bz + by) * 2 + bx) * 2 + h]
+
+    def share_mark(bx, by, bz):
+        return lambda: sib_sem.at[(2 * bz + by) * 2 + bx]
 
     def arrive(dst, sem):
         pltpu.make_async_remote_copy(
             src_ref=dst, dst_ref=dst, send_sem=send_sem.at[0], recv_sem=sem,
             device_id=to_s, device_id_type=MESH).wait_recv()
 
-    def forward(bx, by, bz, device, guards=(), src=None):
-        send(src or place(bx, by, bz), place(bx, by, bz), mark(own_sem, bx, by, bz), device, guards)
+    def forward(bx, by, bz, h, device, guards=(), src=None):
+        send(src or part(bx, by, bz, h), part(bx, by, bz, h), part_mark(bx, by, bz, h), device, guards)
 
     def share(bx, by, bz, guards=(), src=None):
-        send(src or place(bx, by, bz), place(bx, by, bz), mark(sib_sem, bx, by, bz), to_s, guards)
-
-    def take(bx, by, bz):
-        arrive(place(bx, by, bz)(), mark(own_sem, bx, by, bz)())
-
-    def part(bx, by, bz, h):
-        return lambda: buf.at[2 * bz + by, 2 * bx + c, pl.ds(h * half, half)]
+        send(src or place(bx, by, bz), place(bx, by, bz), share_mark(bx, by, bz), to_s, guards)
+
+    def take(bx, by, bz, h):
+        arrive(part(bx, by, bz, h)(), part_mark(bx, by, bz, h)())
 
     def when(guard, body):
         pl.when(guard)(body)
 
-    mine = lambda: cur_ref
-    forward(x, y, z, to_x, src=mine)
-    forward(x, y, z, to_y, src=mine)
-    when(has_up, lambda: forward(x, y, z, to_up, (has_up,), mine))
-    when(has_down, lambda: forward(x, y, z, to_down, (has_down,), mine))
-    share(x, y, z, src=mine)
+    for h in HALVES:
+        mine = lambda h=h: cur_ref.at[pl.ds(h * half, half)]
+        when(has_up, lambda: forward(x, y, z, h, to_up, (has_up,), mine))
+        when(has_down, lambda: forward(x, y, z, h, to_down, (has_down,), mine))
+        forward(x, y, z, h, to_x, src=mine)
+        forward(x, y, z, h, to_y, src=mine)
+    share(x, y, z, src=lambda: cur_ref)
 
     acc[...] = jnp.zeros_like(acc)
 
-    def go_on(bx, by, bz, up, guard):
+    def go_on(bx, by, bz, h, up, guard):
         g, device = (has_up, to_up) if up else (has_down, to_down)
-        when(g, lambda: forward(bx, by, bz, device, (guard, g)))
-
-    def column(up, d):
-        bz = z - d if up else z + d
-        guard = bz >= 0 if up else bz < planes
+        when(g, lambda: forward(bx, by, bz, h, device, (guard, g)))
+
+    def at_plane(up, d):
+        return (z - d, z >= d) if up else (z + d, z + d < planes)
+
+    def column(up, d, h):
+        bz, guard = at_plane(up, d)
 
         def body():
-            take(x, y, bz)
+            take(x, y, bz, h)
             if d < planes - 1:
-                go_on(x, y, bz, up, guard)
-            forward(x, y, bz, to_x, (guard,))
-            forward(x, y, bz, to_y, (guard,))
-            share(x, y, bz, (guard,))
+                go_on(x, y, bz, h, up, guard)
+            forward(x, y, bz, h, to_x, (guard,))
+            forward(x, y, bz, h, to_y, (guard,))
+            if h == 1:
+                share(x, y, bz, (guard,))
 
         when(guard, body)
 
     last = planes - 1 if planes >= 3 else planes
 
-    def diagonal(up, d):
-        bz = z - d if up else z + d
-        guard = bz >= 0 if up else bz < planes
+    def diagonal(up, d, h):
+        bz, guard = at_plane(up, d)
 
         def body():
-            if d < last:
-                take(nx, ny, bz)
-                if d + 1 < last:
-                    go_on(nx, ny, bz, up, guard)
-            else:
-                for h in (0, 1):
-                    arrive(part(nx, ny, bz, h)(), half_sem.at[2 + h])
-            share(nx, ny, bz, (guard,))
+            take(nx, ny, bz, h)
+            if d + 1 < last:
+                go_on(nx, ny, bz, h, up, guard)
+            if h == 1:
+                share(nx, ny, bz, (guard,))
 
         when(guard, body)
 
-    def sides(up, d):
-        bz = z - d if up else z + d
-        guard = bz >= 0 if up else bz < planes
-
-        def body():
-            take(nx, y, bz)
-            if d == last:
-                send(part(nx, y, bz, 0), part(nx, y, bz, 0), lambda: half_sem.at[2], to_y, (guard,))
-            share(nx, y, bz, (guard,))
-            take(x, ny, bz)
-            if d == last:
-                send(part(x, ny, bz, 1), part(x, ny, bz, 1), lambda: half_sem.at[3], to_x, (guard,))
-            share(x, ny, bz, (guard,))
-
-        when(guard, body)
+    def side(bz, guards, turn):
+        take(nx, y, bz, 0)
+        if turn:
+            forward(nx, y, bz, 0, to_y, guards)
+        take(x, ny, bz, 0)
+        take(x, ny, bz, 1)
+        if turn:
+            forward(x, ny, bz, 1, to_x, guards)
+        take(nx, y, bz, 1)
+        share(nx, y, bz, guards)
+        share(x, ny, bz, guards)
+
+    def sides(up, d, h):
+        bz, guard = at_plane(up, d)
+        if h == 0:
+            when(guard, lambda: side(bz, (guard,), d == last))
 
     def multiply(by, bz):
         for bx in (0, 1):
-            arrive(buf.at[2 * bz + by, 2 * bx + 1 - c], mark(sib_sem, bx, by, bz)())
+            arrive(buf.at[2 * bz + by, 2 * bx + 1 - c], share_mark(bx, by, bz)())
         r = 2 * bz + by
         lhs = buf[r].reshape(-1, width)
         acc[pl.ds(PAD, lhs.shape[0]), :] += lax.dot_general(
             lhs, pan[r], (((1,), (1,)), ((), ())), preferred_element_type=jnp.float32)
 
-    def multiply_plane(up, d):
-        bz = z - d if up else z + d
-        guard = bz >= 0 if up else bz < planes
+    def multiply_plane(up, d, h):
+        bz, guard = at_plane(up, d)
+        if h == 1:
+            return
 
         def body():
             @pl.loop(0, 2)
@@ -166,25 +172,19 @@
 
         when(guard, body)
 
-    take(nx, y, z)
-    send(part(nx, y, z, 0), part(nx, y, z, 0), lambda: half_sem.at[0], to_y)
-    share(nx, y, z)
-    take(x, ny, z)
-    send(part(x, ny, z, 1), part(x, ny, z, 1), lambda: half_sem.at[1], to_x)
-    share(x, ny, z)
-    if planes > 1:
-        column(True, 1)
-        column(False, 1)
-    for h in (0, 1):
-        arrive(part(nx, ny, z, h)(), half_sem.at[h])
-    when(has_up, lambda: forward(nx, ny, z, to_up, (has_up,)))
-    when(has_down, lambda: forward(nx, ny, z, to_down, (has_down,)))
-    share(nx, ny, z)
     def both(step, d):
         if 1 <= d < planes:
-            step(True, d)
-            step(False, d)
-
+            for h in HALVES:
+                step(True, d, h)
+                step(False, d, h)
+
+    side(z, (), True)
+    both(column, 1)
+    for h in HALVES:
+        take(nx, ny, z, h)
+        when(has_up, lambda: forward(nx, ny, z, h, to_up, (has_up,)))
+        when(has_down, lambda: forward(nx, ny, z, h, to_down, (has_down,)))
+    share(nx, ny, z)
     both(column, 2)
     if last > 1:
         both(diagonal, 1)
@@ -269,10 +269,9 @@
             pltpu.VMEM((2, PIECES, piece, count), jnp.float32),
             pltpu.VMEM((PIECES, piece, count), jnp.float32),
             pltpu.VMEM((PIECES, piece, count), jnp.float32),
-            dma((24 + 20 * planes + 3 * PIECES,)),
+            dma((24 + 32 * planes + 3 * PIECES,)),
+            dma((4 * rows,)),
             dma((2 * rows,)),
-            dma((2 * rows,)),
-            dma((4,)),
             dma((2 + rows,)),
             dma((2 * PIECES,)),
             dma((PIECES,)),

time: 42.2 us -> 41.8 us (level)
  no operation moved by 1% of the time
where the time goes in v1:
time: 41.8 us; the launch traced here: 41.6 us
  Pallas kernels  39.9 us (95%)
  local copies, waits for them, and re-layouts  1.67 us (4%)
    pallas_call x1, Pallas kernels, fused(): pl.pallas_call(functools.partial(kernel, planes), out_shape=jax.ShapeDtyp...  39.9 us
    unnamed x1, local copies, waits for them, and re-layouts  1.67 us

profile of v1, /device:TPU:0, one launch (start us, length us, event | category | flops | bytes accessed | tf_op | source)
XLA Modules:
  0.0 41.6 jit_solution(3324784209747712719)
XLA Ops:
  0.0 39.9 %shard_map.37 = f32[128,512]{1,0:T(8,128)} custom-call(bf16[128,512]{1,0:T(8,128)(2,1)} %cur_ref.1, bf16[1,512,4096]{2,1,0:T(8,128)(2,1)} %pan_ref.1, f32[128,512]{1,0:T(8,128)} %exc_ref.1), custom_call_target="tpu_custom_call" | custom-call | flops 2147483648 | bytes 4194304 | tf_op jit(solution)/shard_map/pallas_call | solution.py:258
  40.0 1.7 %copy.5 = f32[128,512]{1,0:T(8,128)} copy(f32[128,512]{1,0:T(8,128)} %shard_map.37) | data formatting | bytes 524288

commit v2 on v1

--- a/solution.py
+++ b/solution.py
@@ -160,17 +160,15 @@
         acc[pl.ds(PAD, lhs.shape[0]), :] += lax.dot_general(
             lhs, pan[r], (((1,), (1,)), ((), ())), preferred_element_type=jnp.float32)
 
-    def multiply_plane(up, d, h):
-        bz, guard = at_plane(up, d)
-        if h == 1:
-            return
-
-        def body():
-            @pl.loop(0, 2)
-            def _(by):
-                multiply(by, bz)
-
-        when(guard, body)
+    def multiply_near(up, d, h):
+        bz, guard = at_plane(up, d)
+        if h == 0:
+            when(guard, lambda: multiply(y, bz))
+
+    def multiply_far(up, d, h):
+        bz, guard = at_plane(up, d)
+        if h == 0:
+            when(guard, lambda: multiply(ny, bz))
 
     def both(step, d):
         if 1 <= d < planes:
@@ -180,40 +178,42 @@
 
     side(z, (), True)
     both(column, 1)
+    both(column, 2)
     for h in HALVES:
         take(nx, ny, z, h)
         when(has_up, lambda: forward(nx, ny, z, h, to_up, (has_up,)))
         when(has_down, lambda: forward(nx, ny, z, h, to_down, (has_down,)))
     share(nx, ny, z)
-    both(column, 2)
     if last > 1:
         both(diagonal, 1)
     for load in loads:
         load.wait()
-
-    @pl.loop(0, 2)
-    def _(by):
-        multiply(by, z)
-
+    multiply(y, z)
     both(column, 3)
+    multiply(ny, z)
+    both(sides, 1)
+    both(multiply_near, 1)
     if last > 2:
         both(diagonal, 2)
-    both(sides, 1)
     if last > 1:
-        both(multiply_plane, 1)
+        both(multiply_far, 1)
     for d in range(2, planes):
         if d + 2 < planes:
             both(column, d + 2)
-        if d + 1 < last:
+        if 2 < d + 1 < last:
             both(diagonal, d + 1)
-        both(sides, d)
-        if d == last:
-            if d > 2:
-                both(multiply_plane, d - 1)
+        if d < last or d == 2:
+            both(sides, d)
+        if d < last:
+            if d + 1 == last:
+                both(sides, d + 1)
+            both(multiply_near, d)
+            both(multiply_far, d)
+        else:
+            both(multiply_near, d)
             both(diagonal, d)
-            both(multiply_plane, d)
-        elif d + 1 < last:
-            both(multiply_plane, d)
+            both(multiply_far, d)
+
     piece = steps // PIECES
 
     def shifted(bx, core, p):
@@ -221,15 +221,19 @@
         window = acc[pl.ds(first, piece + 8), :]
         return pltpu.roll(window, piece + lag, 0)[:piece]
 
-    order = [(0, p) for p in range(PIECES)] + [(1, p) for p in range(PIECES)]
-    for j, p in order:
+    def give_piece(j, p):
         give[j, p] = shifted(nx if j == 0 else x, 1 - c, p)
         send(lambda j=j, p=p: give.at[j, p], lambda j=j, p=p: got.at[j, p],
              lambda j=j, p=p: give_sem.at[j * PIECES + p], to_s)
+
+    for p in range(PIECES):
+        give_piece(0, p)
     for p in range(PIECES):
         arrive(got.at[0, p], give_sem.at[p])
         over[p] = shifted(nx, c, p) + got[0, p]
         send(lambda p=p: over.at[p], lambda p=p: landed.at[p], lambda p=p: over_sem.at[p], to_x)
+    for p in range(PIECES):
+        give_piece(1, p)
     for p in range(PIECES):
         arrive(got.at[1, p], give_sem.at[PIECES + p])
         at = pl.ds(p * piece, piece)

time: 41.8 us -> 42.1 us (level)
  no operation moved by 1% of the time
where the time goes in v2:
time: 42.1 us; the launch traced here: 41.9 us
  Pallas kernels  40.2 us (95%)
  local copies, waits for them, and re-layouts  1.67 us (4%)
    pallas_call x1, Pallas kernels, fused(): pl.pallas_call(functools.partial(kernel, planes), out_shape=jax.ShapeDtyp...  40.2 us
    unnamed x1, local copies, waits for them, and re-layouts  1.67 us

profile of v2, /device:TPU:0, one launch (start us, length us, event | category | flops | bytes accessed | tf_op | source)
XLA Modules:
  0.0 41.9 jit_solution(16250177838443096645)
XLA Ops:
  0.0 40.2 %shard_map.37 = f32[128,512]{1,0:T(8,128)} custom-call(bf16[128,512]{1,0:T(8,128)(2,1)} %cur_ref.1, bf16[1,512,4096]{2,1,0:T(8,128)(2,1)} %pan_ref.1, f32[128,512]{1,0:T(8,128)} %exc_ref.1), custom_call_target="tpu_custom_call" | custom-call | flops 2147483648 | bytes 4194304 | tf_op jit(solution)/shard_map/pallas_call | solution.py:262
  40.3 1.7 %copy.5 = f32[128,512]{1,0:T(8,128)} copy(f32[128,512]{1,0:T(8,128)} %shard_map.37) | data formatting | bytes 524288

commit v3 on v1

--- a/solution.py
+++ b/solution.py
@@ -221,16 +221,30 @@
         window = acc[pl.ds(first, piece + 8), :]
         return pltpu.roll(window, piece + lag, 0)[:piece]
 
-    order = [(0, p) for p in range(PIECES)] + [(1, p) for p in range(PIECES)]
-    for j, p in order:
+    def give_piece(j, p):
         give[j, p] = shifted(nx if j == 0 else x, 1 - c, p)
         send(lambda j=j, p=p: give.at[j, p], lambda j=j, p=p: got.at[j, p],
              lambda j=j, p=p: give_sem.at[j * PIECES + p], to_s)
+
+    def finish(group):
+        for guards, make in group:
+            if guards:
+                g = functools.reduce(jnp.logical_and, guards)
+                pl.when(g)(lambda make=make: make().wait_send())
+            else:
+                make().wait_send()
+
+    gathered = len(sent)
+    for p in range(PIECES):
+        give_piece(0, p)
     for p in range(PIECES):
         arrive(got.at[0, p], give_sem.at[p])
         over[p] = shifted(nx, c, p) + got[0, p]
         send(lambda p=p: over.at[p], lambda p=p: landed.at[p], lambda p=p: over_sem.at[p], to_x)
     for p in range(PIECES):
+        give_piece(1, p)
+    finish(sent[:gathered])
+    for p in range(PIECES):
         arrive(got.at[1, p], give_sem.at[PIECES + p])
         at = pl.ds(p * piece, piece)
         exc[at, :] = exc[at, :] - (shifted(x, c, p) + got[1, p])
@@ -239,12 +253,7 @@
         at = pl.ds(p * piece, piece)
         out_ref[at, :] = exc[at, :] - landed[p]
 
-    for guards, make in sent:
-        if guards:
-            g = functools.reduce(jnp.logical_and, guards)
-            pl.when(g)(lambda make=make: make().wait_send())
-        else:
-            make().wait_send()
+    finish(sent[gathered:])
 
 
 def fused(currents, panels, excitation):

time: 41.8 us -> 41.7 us (level)
  no operation moved by 1% of the time
where the time goes in v3:
time: 41.7 us; the launch traced here: 41.5 us
  Pallas kernels  39.9 us (96%)
  local copies, waits for them, and re-layouts  1.67 us (4%)
    pallas_call x1, Pallas kernels, fused(): pl.pallas_call(functools.partial(kernel, planes), out_shape=jax.ShapeDtyp...  39.9 us
    unnamed x1, local copies, waits for them, and re-layouts  1.67 us

profile of v3, /device:TPU:0, one launch (start us, length us, event | category | flops | bytes accessed | tf_op | source)
XLA Modules:
  0.0 41.5 jit_solution(9756570411986282880)
XLA Ops:
  0.0 39.9 %shard_map.37 = f32[128,512]{1,0:T(8,128)} custom-call(bf16[128,512]{1,0:T(8,128)(2,1)} %cur_ref.1, bf16[1,512,4096]{2,1,0:T(8,128)(2,1)} %pan_ref.1, f32[128,512]{1,0:T(8,128)} %exc_ref.1), custom_call_target="tpu_custom_call" | custom-call | flops 2147483648 | bytes 4194304 | tf_op jit(solution)/shard_map/pallas_call | solution.py:267
  39.9 1.7 %copy.5 = f32[128,512]{1,0:T(8,128)} copy(f32[128,512]{1,0:T(8,128)} %shard_map.37) | data formatting | bytes 524288

commit v4 on v2

--- a/solution.py
+++ b/solution.py
@@ -128,20 +128,20 @@
 
         def body():
             take(nx, ny, bz, h)
-            if d + 1 < last:
+            if d + 1 < last or (d + 1 == last and h == 1 and last < planes):
                 go_on(nx, ny, bz, h, up, guard)
             if h == 1:
                 share(nx, ny, bz, (guard,))
 
         when(guard, body)
 
-    def side(bz, guards, turn):
+    def side(bz, guards, over_x, over_y):
         take(nx, y, bz, 0)
-        if turn:
+        if over_y:
             forward(nx, y, bz, 0, to_y, guards)
         take(x, ny, bz, 0)
         take(x, ny, bz, 1)
-        if turn:
+        if over_x:
             forward(x, ny, bz, 1, to_x, guards)
         take(nx, y, bz, 1)
         share(nx, y, bz, guards)
@@ -150,7 +150,7 @@
     def sides(up, d, h):
         bz, guard = at_plane(up, d)
         if h == 0:
-            when(guard, lambda: side(bz, (guard,), d == last))
+            when(guard, lambda: side(bz, (guard,), False, d == last))
 
     def multiply(by, bz):
         for bx in (0, 1):
@@ -176,7 +176,7 @@
                 step(True, d, h)
                 step(False, d, h)
 
-    side(z, (), True)
+    side(z, (), True, True)
     both(column, 1)
     both(column, 2)
     for h in HALVES:
@@ -226,6 +226,15 @@
         send(lambda j=j, p=p: give.at[j, p], lambda j=j, p=p: got.at[j, p],
              lambda j=j, p=p: give_sem.at[j * PIECES + p], to_s)
 
+    def finish(group):
+        for guards, make in group:
+            if guards:
+                g = functools.reduce(jnp.logical_and, guards)
+                pl.when(g)(lambda make=make: make().wait_send())
+            else:
+                make().wait_send()
+
+    gathered = len(sent)
     for p in range(PIECES):
         give_piece(0, p)
     for p in range(PIECES):
@@ -234,6 +243,7 @@
         send(lambda p=p: over.at[p], lambda p=p: landed.at[p], lambda p=p: over_sem.at[p], to_x)
     for p in range(PIECES):
         give_piece(1, p)
+    finish(sent[:gathered])
     for p in range(PIECES):
         arrive(got.at[1, p], give_sem.at[PIECES + p])
         at = pl.ds(p * piece, piece)
@@ -243,12 +253,7 @@
         at = pl.ds(p * piece, piece)
         out_ref[at, :] = exc[at, :] - landed[p]
 
-    for guards, make in sent:
-        if guards:
-            g = functools.reduce(jnp.logical_and, guards)
-            pl.when(g)(lambda make=make: make().wait_send())
-        else:
-            make().wait_send()
+    finish(sent[gathered:])
 
 
 def fused(currents, panels, excitation):

time: 42.1 us -> 41.2 us (0.979)
  Pallas kernels: 40.2 us -> 39.4 us
    pallas_call x1, Pallas kernels: 40.2 us -> 39.4 us  [fused(): pl.pallas_call(functools.partial(kernel, planes), out_shape=jax.ShapeDtyp...]
where the time goes in v4:
time: 41.2 us; the launch traced here: 41.1 us
  Pallas kernels  39.4 us (96%)
  local copies, waits for them, and re-layouts  1.67 us (4%)
    pallas_call x1, Pallas kernels, fused(): pl.pallas_call(functools.partial(kernel, planes), out_shape=jax.ShapeDtyp...  39.4 us
    unnamed x1, local copies, waits for them, and re-layouts  1.67 us

profile of v4, /device:TPU:0, one launch (start us, length us, event | category | flops | bytes accessed | tf_op | source)
XLA Modules:
  0.0 41.1 jit_solution(15309655765121919436)
XLA Ops:
  0.0 39.4 %shard_map.37 = f32[128,512]{1,0:T(8,128)} custom-call(bf16[128,512]{1,0:T(8,128)(2,1)} %cur_ref.1, bf16[1,512,4096]{2,1,0:T(8,128)(2,1)} %pan_ref.1, f32[128,512]{1,0:T(8,128)} %exc_ref.1), custom_call_target="tpu_custom_call" | custom-call | flops 2147483648 | bytes 4194304 | tf_op jit(solution)/shard_map/pallas_call | solution.py:267
  39.4 1.7 %copy.5 = f32[128,512]{1,0:T(8,128)} copy(f32[128,512]{1,0:T(8,128)} %shard_map.37) | data formatting | bytes 524288

commit v5 on v4

--- a/solution.py
+++ b/solution.py
@@ -135,22 +135,20 @@
 
         when(guard, body)
 
-    def side(bz, guards, over_x, over_y):
-        take(nx, y, bz, 0)
-        if over_y:
-            forward(nx, y, bz, 0, to_y, guards)
+    def side(bz, guards, halves):
+        for h in HALVES:
+            take(nx, y, bz, h)
+            if h in halves:
+                forward(nx, y, bz, h, to_y, guards)
+        share(nx, y, bz, guards)
         take(x, ny, bz, 0)
         take(x, ny, bz, 1)
-        if over_x:
-            forward(x, ny, bz, 1, to_x, guards)
-        take(nx, y, bz, 1)
-        share(nx, y, bz, guards)
         share(x, ny, bz, guards)
 
     def sides(up, d, h):
         bz, guard = at_plane(up, d)
         if h == 0:
-            when(guard, lambda: side(bz, (guard,), False, d == last))
+            when(guard, lambda: side(bz, (guard,), (0,) if d == last else ()))
 
     def multiply(by, bz):
         for bx in (0, 1):
@@ -176,7 +174,7 @@
                 step(True, d, h)
                 step(False, d, h)
 
-    side(z, (), True, True)
+    side(z, (), HALVES)
     both(column, 1)
     both(column, 2)
     for h in HALVES:

time: 41.2 us -> 41.5 us (level)
  no operation moved by 1% of the time
where the time goes in v5:
time: 41.5 us; the launch traced here: 41.4 us
  Pallas kernels  39.7 us (96%)
  local copies, waits for them, and re-layouts  1.67 us (4%)
    pallas_call x1, Pallas kernels, fused(): pl.pallas_call(functools.partial(kernel, planes), out_shape=jax.ShapeDtyp...  39.7 us
    unnamed x1, local copies, waits for them, and re-layouts  1.67 us

profile of v5, /device:TPU:0, one launch (start us, length us, event | category | flops | bytes accessed | tf_op | source)
XLA Modules:
  0.0 41.4 jit_solution(15283212976223700459)
XLA Ops:
  0.0 39.7 %shard_map.37 = f32[128,512]{1,0:T(8,128)} custom-call(bf16[128,512]{1,0:T(8,128)(2,1)} %cur_ref.1, bf16[1,512,4096]{2,1,0:T(8,128)(2,1)} %pan_ref.1, f32[128,512]{1,0:T(8,128)} %exc_ref.1), custom_call_target="tpu_custom_call" | custom-call | flops 2147483648 | bytes 4194304 | tf_op jit(solution)/shard_map/pallas_call | solution.py:265
  39.7 1.7 %copy.5 = f32[128,512]{1,0:T(8,128)} copy(f32[128,512]{1,0:T(8,128)} %shard_map.37) | data formatting | bytes 524288

commit v6 on v4

--- a/solution.py
+++ b/solution.py
@@ -26,6 +26,9 @@
     to_s = (2 * x + 1 - c, row)
     to_up, to_down = (lag, row + 2), (lag, row - 2)
     has_up, has_down = z + 1 < planes, z >= 1
+    direct = planes >= 4
+    at_end = jnp.logical_or(z == 0, z == planes - 1)
+    to_end = (lag, 2 * (planes - 1 - z) + y)
 
     barrier = pltpu.get_barrier_semaphore()
 
@@ -37,6 +40,8 @@
     greet(to_y)
     pl.when(has_up)(lambda: greet(to_up))
     pl.when(has_down)(lambda: greet(to_down))
+    if direct:
+        pl.when(at_end)(lambda: greet(to_end))
 
     loads = [pltpu.make_async_copy(cur_ref, buf.at[row, lag], load_sem.at[0]),
              pltpu.make_async_copy(exc_ref, exc, load_sem.at[1])]
@@ -46,7 +51,8 @@
     for load in loads:
         load.start()
 
-    pl.semaphore_wait(barrier, 3 + has_up.astype(jnp.int32) + has_down.astype(jnp.int32))
+    greeted = 3 + has_up.astype(jnp.int32) + has_down.astype(jnp.int32)
+    pl.semaphore_wait(barrier, greeted + at_end.astype(jnp.int32) if direct else greeted)
 
     sent = []
 
@@ -94,6 +100,8 @@
         mine = lambda h=h: cur_ref.at[pl.ds(h * half, half)]
         when(has_up, lambda: forward(x, y, z, h, to_up, (has_up,), mine))
         when(has_down, lambda: forward(x, y, z, h, to_down, (has_down,), mine))
+        if direct:
+            when(at_end, lambda: forward(x, y, z, h, to_end, (at_end,), mine))
         forward(x, y, z, h, to_x, src=mine)
         forward(x, y, z, h, to_y, src=mine)
     share(x, y, z, src=lambda: cur_ref)
@@ -112,7 +120,7 @@
 
         def body():
             take(x, y, bz, h)
-            if d < planes - 1:
+            if d < planes - (2 if direct else 1):
                 go_on(x, y, bz, h, up, guard)
             forward(x, y, bz, h, to_x, (guard,))
             forward(x, y, bz, h, to_y, (guard,))
@@ -178,7 +186,8 @@
 
     side(z, (), True, True)
     both(column, 1)
-    both(column, 2)
+    for d in range(2, planes):
+        both(column, d)
     for h in HALVES:
         take(nx, ny, z, h)
         when(has_up, lambda: forward(nx, ny, z, h, to_up, (has_up,)))
@@ -189,30 +198,19 @@
     for load in loads:
         load.wait()
     multiply(y, z)
-    both(column, 3)
+    both(sides, 1)
     multiply(ny, z)
-    both(sides, 1)
-    both(multiply_near, 1)
-    if last > 2:
-        both(diagonal, 2)
-    if last > 1:
-        both(multiply_far, 1)
+    for d in range(2, last):
+        both(diagonal, d)
     for d in range(2, planes):
-        if d + 2 < planes:
-            both(column, d + 2)
-        if 2 < d + 1 < last:
-            both(diagonal, d + 1)
-        if d < last or d == 2:
-            both(sides, d)
-        if d < last:
-            if d + 1 == last:
-                both(sides, d + 1)
-            both(multiply_near, d)
-            both(multiply_far, d)
-        else:
-            both(multiply_near, d)
-            both(diagonal, d)
-            both(multiply_far, d)
+        both(sides, d)
+        both(multiply_near, d - 1)
+        both(multiply_far, d - 1)
+    if planes > 1:
+        both(multiply_near, planes - 1)
+        if last < planes:
+            both(diagonal, last)
+        both(multiply_far, planes - 1)
 
     piece = steps // PIECES
 
@@ -278,7 +276,7 @@
             pltpu.VMEM((2, PIECES, piece, count), jnp.float32),
             pltpu.VMEM((PIECES, piece, count), jnp.float32),
             pltpu.VMEM((PIECES, piece, count), jnp.float32),
-            dma((24 + 32 * planes + 3 * PIECES,)),
+            dma((26 + 32 * planes + 3 * PIECES,)),
             dma((4 * rows,)),
             dma((2 * rows,)),
             dma((2 + rows,)),

time: 41.2 us -> 42.6 us (1.034)
  Pallas kernels: 39.4 us -> 40.7 us
    pallas_call x1, Pallas kernels: 39.4 us -> 40.7 us  [fused(): pl.pallas_call(functools.partial(kernel, planes), out_shape=jax.ShapeDtyp...]
where the time goes in v6:
time: 42.6 us; the launch traced here: 42.4 us
  Pallas kernels  40.7 us (96%)
  local copies, waits for them, and re-layouts  1.67 us (4%)
    pallas_call x1, Pallas kernels, fused(): pl.pallas_call(functools.partial(kernel, planes), out_shape=jax.ShapeDtyp...  40.7 us
    unnamed x1, local copies, waits for them, and re-layouts  1.67 us

profile of v6, /device:TPU:0, one launch (start us, length us, event | category | flops | bytes accessed | tf_op | source)
XLA Modules:
  0.0 42.4 jit_solution(5083730099907263925)
XLA Ops:
  0.0 40.7 %shard_map.37 = f32[128,512]{1,0:T(8,128)} custom-call(bf16[128,512]{1,0:T(8,128)(2,1)} %cur_ref.1, bf16[1,512,4096]{2,1,0:T(8,128)(2,1)} %pan_ref.1, f32[128,512]{1,0:T(8,128)} %exc_ref.1), custom_call_target="tpu_custom_call" | custom-call | flops 2147483648 | bytes 4194304 | tf_op jit(solution)/shard_map/pallas_call | solution.py:265
  40.8 1.7 %copy.5 = f32[128,512]{1,0:T(8,128)} copy(f32[128,512]{1,0:T(8,128)} %shard_map.37) | data formatting | bytes 524288

commit v7 on v6

--- a/solution.py
+++ b/solution.py
@@ -167,6 +167,24 @@
         lhs = buf[r].reshape(-1, width)
         acc[pl.ds(PAD, lhs.shape[0]), :] += lax.dot_general(
             lhs, pan[r], (((1,), (1,)), ((), ())), preferred_element_type=jnp.float32)
+
+    def multiply_rows(by, bz, bx):
+        arrive(buf.at[2 * bz + by, 2 * bx + 1 - c], share_mark(bx, by, bz)())
+        r = 2 * bz + by
+        lhs = buf[r, pl.ds(2 * bx, 2)].reshape(-1, width)
+        at = pl.ds(pl.multiple_of(PAD + 2 * steps * bx, 8), 2 * steps)
+        acc[at, :] += lax.dot_general(
+            lhs, pan[r], (((1,), (1,)), ((), ())), preferred_element_type=jnp.float32)
+
+    def multiply_own(up, d, h):
+        bz, guard = at_plane(up, d)
+        if h == 0:
+            when(guard, lambda: multiply_rows(ny, bz, x))
+
+    def multiply_other(up, d, h):
+        bz, guard = at_plane(up, d)
+        if h == 0:
+            when(guard, lambda: multiply_rows(ny, bz, nx))
 
     def multiply_near(up, d, h):
         bz, guard = at_plane(up, d)
@@ -208,9 +226,10 @@
         both(multiply_far, d - 1)
     if planes > 1:
         both(multiply_near, planes - 1)
+        both(multiply_own, planes - 1)
         if last < planes:
             both(diagonal, last)
-        both(multiply_far, planes - 1)
+        both(multiply_other, planes - 1)
 
     piece = steps // PIECES
 

time: 42.6 us -> 42.4 us (level)
  no operation moved by 1% of the time
where the time goes in v7:
time: 42.4 us; the launch traced here: 42.3 us
  Pallas kernels  40.6 us (96%)
  local copies, waits for them, and re-layouts  1.67 us (4%)
    pallas_call x1, Pallas kernels, fused(): pl.pallas_call(functools.partial(kernel, planes), out_shape=jax.ShapeDtyp...  40.6 us
    unnamed x1, local copies, waits for them, and re-layouts  1.67 us

profile of v7, /device:TPU:0, one launch (start us, length us, event | category | flops | bytes accessed | tf_op | source)
XLA Modules:
  0.0 42.3 jit_solution(8194126892740719550)
XLA Ops:
  0.0 40.6 %shard_map.37 = f32[128,512]{1,0:T(8,128)} custom-call(bf16[128,512]{1,0:T(8,128)(2,1)} %cur_ref.1, bf16[1,512,4096]{2,1,0:T(8,128)(2,1)} %pan_ref.1, f32[128,512]{1,0:T(8,128)} %exc_ref.1), custom_call_target="tpu_custom_call" | custom-call | flops 2147483648 | bytes 4194304 | tf_op jit(solution)/shard_map/pallas_call | solution.py:284
  40.6 1.7 %copy.5 = f32[128,512]{1,0:T(8,128)} copy(f32[128,512]{1,0:T(8,128)} %shard_map.37) | data formatting | bytes 524288

commit v8 on v4

--- a/solution.py
+++ b/solution.py
@@ -14,7 +14,7 @@
 
 
 def kernel(planes, cur_ref, pan_ref, exc_ref, out_ref, buf, pan, exc, acc, give, got, over, landed,
-           send_sem, own_sem, sib_sem, load_sem, give_sem, over_sem):
+           send_sem, own_sem, sib_sem, load_sem, give_sem, over_sem, store_sem):
     lag, row = lax.axis_index("lag"), lax.axis_index("row")
     x, c = lag // 2, lag % 2
     z, y = row // 2, row % 2
@@ -26,6 +26,9 @@
     to_s = (2 * x + 1 - c, row)
     to_up, to_down = (lag, row + 2), (lag, row - 2)
     has_up, has_down = z + 1 < planes, z >= 1
+    direct = planes >= 4
+    at_end = jnp.logical_or(z == 0, z == planes - 1)
+    to_end = (lag, 2 * (planes - 1 - z) + y)
 
     barrier = pltpu.get_barrier_semaphore()
 
@@ -37,6 +40,8 @@
     greet(to_y)
     pl.when(has_up)(lambda: greet(to_up))
     pl.when(has_down)(lambda: greet(to_down))
+    if direct:
+        pl.when(at_end)(lambda: greet(to_end))
 
     loads = [pltpu.make_async_copy(cur_ref, buf.at[row, lag], load_sem.at[0]),
              pltpu.make_async_copy(exc_ref, exc, load_sem.at[1])]
@@ -46,7 +51,8 @@
     for load in loads:
         load.start()
 
-    pl.semaphore_wait(barrier, 3 + has_up.astype(jnp.int32) + has_down.astype(jnp.int32))
+    greeted = 3 + has_up.astype(jnp.int32) + has_down.astype(jnp.int32)
+    pl.semaphore_wait(barrier, greeted + at_end.astype(jnp.int32) if direct else greeted)
 
     sent = []
 
@@ -96,6 +102,8 @@
         when(has_down, lambda: forward(x, y, z, h, to_down, (has_down,), mine))
         forward(x, y, z, h, to_x, src=mine)
         forward(x, y, z, h, to_y, src=mine)
+        if direct:
+            when(at_end, lambda: forward(x, y, z, h, to_end, (at_end,), mine))
     share(x, y, z, src=lambda: cur_ref)
 
     acc[...] = jnp.zeros_like(acc)
@@ -112,7 +120,7 @@
 
         def body():
             take(x, y, bz, h)
-            if d < planes - 1:
+            if d < planes - (2 if direct else 1):
                 go_on(x, y, bz, h, up, guard)
             forward(x, y, bz, h, to_x, (guard,))
             forward(x, y, bz, h, to_y, (guard,))
@@ -248,12 +256,17 @@
         arrive(got.at[1, p], give_sem.at[PIECES + p])
         at = pl.ds(p * piece, piece)
         exc[at, :] = exc[at, :] - (shifted(x, c, p) + got[1, p])
+    stores = []
     for p in range(PIECES):
         arrive(landed.at[p], over_sem.at[p])
         at = pl.ds(p * piece, piece)
-        out_ref[at, :] = exc[at, :] - landed[p]
+        exc[at, :] = exc[at, :] - landed[p]
+        stores.append(pltpu.make_async_copy(exc.at[at], out_ref.at[at], store_sem.at[p]))
+        stores[-1].start()
 
     finish(sent[gathered:])
+    for store in stores:
+        store.wait()
 
 
 def fused(currents, panels, excitation):
@@ -268,7 +281,7 @@
         functools.partial(kernel, planes),
         out_shape=jax.ShapeDtypeStruct(excitation.shape, jnp.float32),
         in_specs=[hbm_spec] * 3,
-        out_specs=pl.BlockSpec(memory_space=pltpu.VMEM),
+        out_specs=hbm_spec,
         scratch_shapes=[
             pltpu.VMEM((rows, lags, steps, width), jnp.bfloat16),
             pltpu.VMEM((rows, count, width), jnp.bfloat16),
@@ -278,11 +291,12 @@
             pltpu.VMEM((2, PIECES, piece, count), jnp.float32),
             pltpu.VMEM((PIECES, piece, count), jnp.float32),
             pltpu.VMEM((PIECES, piece, count), jnp.float32),
-            dma((24 + 32 * planes + 3 * PIECES,)),
+            dma((26 + 32 * planes + 3 * PIECES,)),
             dma((4 * rows,)),
             dma((2 * rows,)),
             dma((2 + rows,)),
             dma((2 * PIECES,)),
+            dma((PIECES,)),
             dma((PIECES,)),
         ],
         compiler_params=pltpu.CompilerParams(

time: 41.2 us -> 41.4 us (level)
  no operation moved by 1% of the time
where the time goes in v8:
time: 41.4 us; the launch traced here: 41.2 us
  Pallas kernels  39.6 us (96%)
  local copies, waits for them, and re-layouts  1.67 us (4%)
    pallas_call x1, Pallas kernels, fused(): pl.pallas_call(functools.partial(kernel, planes), out_shape=jax.ShapeDtyp...  39.6 us
    unnamed x1, local copies, waits for them, and re-layouts  1.67 us

profile of v8, /device:TPU:0, one launch (start us, length us, event | category | flops | bytes accessed | tf_op | source)
XLA Modules:
  0.0 41.2 jit_solution(17954504760809034582)
XLA Ops:
  0.0 39.6 %shard_map.37 = f32[128,512]{1,0:T(8,128)} custom-call(bf16[128,512]{1,0:T(8,128)(2,1)} %cur_ref.1, bf16[1,512,4096]{2,1,0:T(8,128)(2,1)} %pan_ref.1, f32[128,512]{1,0:T(8,128)} %exc_ref.1), custom_call_target="tpu_custom_call" | custom-call | flops 2147483648 | bytes 4194304 | tf_op jit(solution)/shard_map/pallas_call | solution.py:280
  39.6 1.7 %copy.5 = f32[128,512]{1,0:T(8,128)} copy(f32[128,512]{1,0:T(8,128)} %shard_map.37) | data formatting | bytes 524288

commit v9 on v8

--- a/solution.py
+++ b/solution.py
@@ -136,7 +136,7 @@
 
         def body():
             take(nx, ny, bz, h)
-            if d + 1 < last or (d + 1 == last and h == 1 and last < planes):
+            if d + 1 < last:
                 go_on(nx, ny, bz, h, up, guard)
             if h == 1:
                 share(nx, ny, bz, (guard,))
@@ -158,7 +158,7 @@
     def sides(up, d, h):
         bz, guard = at_plane(up, d)
         if h == 0:
-            when(guard, lambda: side(bz, (guard,), False, d == last))
+            when(guard, lambda: side(bz, (guard,), d == last, d == last))
 
     def multiply(by, bz):
         for bx in (0, 1):
@@ -187,6 +187,7 @@
     side(z, (), True, True)
     both(column, 1)
     both(column, 2)
+    both(column, 3)
     for h in HALVES:
         take(nx, ny, z, h)
         when(has_up, lambda: forward(nx, ny, z, h, to_up, (has_up,)))
@@ -197,7 +198,6 @@
     for load in loads:
         load.wait()
     multiply(y, z)
-    both(column, 3)
     multiply(ny, z)
     both(sides, 1)
     both(multiply_near, 1)

time: 41.4 us -> 41.4 us (level)
  no operation moved by 1% of the time
where the time goes in v9:
time: 41.4 us; the launch traced here: 41.3 us
  Pallas kernels  39.6 us (96%)
  local copies, waits for them, and re-layouts  1.67 us (4%)
    pallas_call x1, Pallas kernels, fused(): pl.pallas_call(functools.partial(kernel, planes), out_shape=jax.ShapeDtyp...  39.6 us
    unnamed x1, local copies, waits for them, and re-layouts  1.67 us

profile of v9, /device:TPU:0, one launch (start us, length us, event | category | flops | bytes accessed | tf_op | source)
XLA Modules:
  0.0 41.3 jit_solution(7341212523188501911)
XLA Ops:
  0.0 39.6 %shard_map.37 = f32[128,512]{1,0:T(8,128)} custom-call(bf16[128,512]{1,0:T(8,128)(2,1)} %cur_ref.1, bf16[1,512,4096]{2,1,0:T(8,128)(2,1)} %pan_ref.1, f32[128,512]{1,0:T(8,128)} %exc_ref.1), custom_call_target="tpu_custom_call" | custom-call | flops 2147483648 | bytes 4194304 | tf_op jit(solution)/shard_map/pallas_call | solution.py:280
  39.6 1.7 %copy.5 = f32[128,512]{1,0:T(8,128)} copy(f32[128,512]{1,0:T(8,128)} %shard_map.37) | data formatting | bytes 524288

commit v10 on v8

--- a/solution.py
+++ b/solution.py
@@ -26,9 +26,6 @@
     to_s = (2 * x + 1 - c, row)
     to_up, to_down = (lag, row + 2), (lag, row - 2)
     has_up, has_down = z + 1 < planes, z >= 1
-    direct = planes >= 4
-    at_end = jnp.logical_or(z == 0, z == planes - 1)
-    to_end = (lag, 2 * (planes - 1 - z) + y)
 
     barrier = pltpu.get_barrier_semaphore()
 
@@ -40,8 +37,6 @@
     greet(to_y)
     pl.when(has_up)(lambda: greet(to_up))
     pl.when(has_down)(lambda: greet(to_down))
-    if direct:
-        pl.when(at_end)(lambda: greet(to_end))
 
     loads = [pltpu.make_async_copy(cur_ref, buf.at[row, lag], load_sem.at[0]),
              pltpu.make_async_copy(exc_ref, exc, load_sem.at[1])]
@@ -51,8 +46,7 @@
     for load in loads:
         load.start()
 
-    greeted = 3 + has_up.astype(jnp.int32) + has_down.astype(jnp.int32)
-    pl.semaphore_wait(barrier, greeted + at_end.astype(jnp.int32) if direct else greeted)
+    pl.semaphore_wait(barrier, 3 + has_up.astype(jnp.int32) + has_down.astype(jnp.int32))
 
     sent = []
 
@@ -102,8 +96,6 @@
         when(has_down, lambda: forward(x, y, z, h, to_down, (has_down,), mine))
         forward(x, y, z, h, to_x, src=mine)
         forward(x, y, z, h, to_y, src=mine)
-        if direct:
-            when(at_end, lambda: forward(x, y, z, h, to_end, (at_end,), mine))
     share(x, y, z, src=lambda: cur_ref)
 
     acc[...] = jnp.zeros_like(acc)
@@ -120,7 +112,7 @@
 
         def body():
             take(x, y, bz, h)
-            if d < planes - (2 if direct else 1):
+            if d < planes - 1:
                 go_on(x, y, bz, h, up, guard)
             forward(x, y, bz, h, to_x, (guard,))
             forward(x, y, bz, h, to_y, (guard,))

time: 41.4 us -> 41.2 us (level)
  no operation moved by 1% of the time
where the time goes in v10:
time: 41.2 us; the launch traced here: 41 us
  Pallas kernels  39.3 us (95%)
  local copies, waits for them, and re-layouts  1.67 us (4%)
    pallas_call x1, Pallas kernels, fused(): pl.pallas_call(functools.partial(kernel, planes), out_shape=jax.ShapeDtyp...  39.3 us
    unnamed x1, local copies, waits for them, and re-layouts  1.67 us

profile of v10, /device:TPU:0, one launch (start us, length us, event | category | flops | bytes accessed | tf_op | source)
XLA Modules:
  0.0 41.0 jit_solution(17133705461842650995)
XLA Ops:
  0.0 39.3 %shard_map.37 = f32[128,512]{1,0:T(8,128)} custom-call(bf16[128,512]{1,0:T(8,128)(2,1)} %cur_ref.1, bf16[1,512,4096]{2,1,0:T(8,128)(2,1)} %pan_ref.1, f32[128,512]{1,0:T(8,128)} %exc_ref.1), custom_call_target="tpu_custom_call" | custom-call | flops 2147483648 | bytes 4194304 | tf_op jit(solution)/shard_map/pallas_call | solution.py:272
  39.3 1.7 %copy.5 = f32[128,512]{1,0:T(8,128)} copy(f32[128,512]{1,0:T(8,128)} %shard_map.37) | data formatting | bytes 524288
